TPU v7x, 256 devices: a whole 4x4x8 slice. The times are simulated.
256 devices in a mesh: table: 32 (over z, x), task: 4 (over y), fsdp: 2 (over core).
Axes of the slice: x: 4, y: 4, z: 8, core: 2. Of those that a mesh axis runs over, the one named last changes fastest.
Arguments:
- raw_ids: int32 [16384, 4, 16], P(('table', 'fsdp'), 'task'), may hold values from 0 to 524287, as said below
- bag_len: int32 [16384, 4], P(('table', 'fsdp'), 'task'), may hold values from 1 to 16, as said below
- labels: int32 [16384, 4], P(('table', 'fsdp'), 'task'), may hold values 0 or 1
- emb_table: bfloat16 [4, 262144, 128], P('task', ('table', 'fsdp')), may hold values from -6 to 6
- bucket_map: int32 [4, 524288], P('task', ('table', 'fsdp')), may hold values from 0 to 4095, as said below
- spec_weight: bfloat16 [4, 512, 4096], P('task', 'fsdp'), may hold values from -0.25 to 0.25
- shared_weight: bfloat16 [4, 512, 4096], P('task', 'fsdp'), may hold values from -0.25 to 0.25
- gate_weight: bfloat16 [4, 512, 5], replicated, may hold values from -1 to 1
- tower_weight: bfloat16 [4, 4096, 256], P('task', 'fsdp'), may hold values from -0.09375 to 0.09375
- head_vector: bfloat16 [4, 256], P('task'), may hold values from -1.5 to 1.5
Outputs:
- logits: float32 [16384, 4], P(('table', 'fsdp'), 'task')
- table_grad: float32 [4, 262144, 128], P('task', ('table', 'fsdp'))
Inputs may be any that keep to these rules, and one draw needn't show every extreme that they name: `raw_ids`: raw id r belongs to block r // 8192. For each field, the samples of one device along table and fsdp name raw ids of one block in exactly 192 live slots and in no dead slot; that block is the same for all devices of a field. Counting all 16 slots of every bag, they name every other block at most 192 times, the remaining slots spread as evenly as possible over the other blocks. `bag_len`: most bags are nearly full; some hold a single live slot. bucket_map[f, r] is a row within the block of r. In each block and field, the rows from 16 up are named by exactly one raw id each; all other raw ids of the block name rows below 16, the shared default buckets.
All inputs are finite; a program needn't handle non-finite values. No bound on the sum of `labels` on one device may be relied on, other than what follows from the above.
Results may differ from a plain program's by a relative error of at most 0.02.
Values may be sent and summed in bfloat16 or wider, within the bound.
No kernel may reach another device: no remote copies, remote signals or barrier semaphores. Data moves between devices by JAX's collectives and lax.ppermute only.
A program may use at most 128 MiB of HBM per device.

v0:
```python
import jax
import jax.numpy as jnp
from jax import lax
from jax.sharding import PartitionSpec as P

loss_scale = 1024.0
highest = lax.Precision.HIGHEST
contract_last = (((1,), (1,)), ((), ()))


def swish_slope(value):
    sigmoid_val = jax.nn.sigmoid(value)
    return sigmoid_val * (1.0 + value * (1.0 - sigmoid_val))


def rounded(value):
    return lax.optimization_barrier(value.astype(jnp.bfloat16)).astype(jnp.float32)


def gate_softmax(scores):
    raised = jnp.exp(scores)
    return raised / jnp.sum(raised, axis=-1, keepdims=True)


def local(
    raw_ids,
    bag_len,
    labels,
    emb_table,
    bucket_map,
    spec_weight,
    shared_weight,
    gate_weight,
    tower_weight,
    head_vector,
):
    owners = lax.axis_size(("table", "fsdp"))
    task_index = lax.axis_index("task")
    sample_count = raw_ids.shape[0]
    slot_count = raw_ids.shape[2]
    lookups = sample_count * slot_count
    capacity = 3 * lookups // owners
    raw_block = bucket_map.shape[1]
    rows_dev = emb_table.shape[1]
    emb_width = emb_table.shape[2]
    flat_ids = raw_ids.reshape(lookups)
    live_slot = (jnp.arange(slot_count, dtype=jnp.int32)[None, :] < bag_len).reshape(lookups)
    owner_of = flat_ids // raw_block
    local_raw = flat_ids - owner_of * raw_block
    owner_hits = (owner_of[:, None] == jnp.arange(owners, dtype=jnp.int32)[None, :]).astype(
        jnp.int32
    )
    slot_rank = jnp.sum((jnp.cumsum(owner_hits, axis=0) - 1) * owner_hits, axis=1)
    slot_index = owner_of * capacity + slot_rank
    sample_of = jnp.arange(lookups, dtype=jnp.int32) // slot_count
    request = (
        jnp.full((owners * capacity,), -1, jnp.int32)
        .at[slot_index]
        .set(jnp.where(live_slot, local_raw, -1))
        .reshape(owners, capacity)
    )
    row_map = bucket_map[0]
    shard_rows = emb_table[0]
    bag_count = bag_len[:, 0].astype(jnp.float32)
    asked = lax.all_to_all(request, ("table", "fsdp"), split_axis=0, concat_axis=0, tiled=True)
    known = asked >= 0
    mapped_rows = jnp.where(known, row_map[jnp.maximum(asked, 0)], 0)
    fetched = jnp.where(known[..., None], shard_rows[mapped_rows], jnp.zeros((), jnp.bfloat16))
    returned_rows = lax.all_to_all(
        fetched, ("table", "fsdp"), split_axis=0, concat_axis=0, tiled=True
    )
    picked = returned_rows.reshape(owners * capacity, emb_width)[slot_index]
    picked = jnp.where(live_slot[:, None], picked.astype(jnp.float32), 0.0)
    summed = jnp.sum(picked.reshape(sample_count, slot_count, emb_width), axis=1)
    pooled = (summed / bag_count[:, None]).astype(jnp.bfloat16)
    features = lax.all_gather(pooled, "task", axis=1, tiled=True)
    gate_own = lax.dynamic_index_in_dim(gate_weight, task_index, 0, keepdims=False)
    targets = labels[:, 0].astype(jnp.float32)
    head_row = head_vector[0].astype(jnp.float32)
    spec_full, shared_full, tower_own = (
        lax.all_gather(spec_weight[0], "fsdp", axis=0, tiled=True),
        lax.all_gather(shared_weight[0], "fsdp", axis=0, tiled=True),
        lax.all_gather(tower_weight[0], "fsdp", axis=0, tiled=True),
    )
    spec_input = jnp.dot(features, spec_full, preferred_element_type=jnp.float32)
    shared_input = jnp.dot(features, shared_full, preferred_element_type=jnp.float32)
    spec_out = jax.nn.silu(spec_input).astype(jnp.bfloat16)
    shared_out = jax.nn.silu(shared_input).astype(jnp.bfloat16)
    spec_proj = jnp.dot(spec_out, tower_own, preferred_element_type=jnp.float32)
    gate_mix = gate_softmax(jnp.dot(features, gate_own, preferred_element_type=jnp.float32))
    shared_all = lax.all_gather(shared_out[None], "task", axis=0, tiled=True)
    shared_proj = jnp.einsum(
        "ksd,dh->ksh", shared_all, tower_own, preferred_element_type=jnp.float32
    )
    tower_pre = gate_mix[:, 0:1] * spec_proj + jnp.sum(
        gate_mix[:, 1:].T[:, :, None] * shared_proj, axis=0
    )
    tower_act = jax.nn.silu(tower_pre)
    logit_own = jnp.sum(tower_act * head_row[None, :], axis=1)
    logit_grad = loss_scale * (jax.nn.sigmoid(logit_own) - targets)
    pre_grad = (logit_grad[:, None] * head_row[None, :] * swish_slope(tower_pre)).astype(
        jnp.bfloat16
    )
    pre_wide = pre_grad.astype(jnp.float32)
    gate_grad = jnp.concatenate(
        [
            jnp.sum(pre_wide * spec_proj, axis=1, keepdims=True),
            jnp.sum(pre_wide[None] * shared_proj, axis=2).T,
        ],
        axis=1,
    )
    back_grad = lax.dot_general(
        pre_grad, tower_own, contract_last, preferred_element_type=jnp.float32
    )
    spec_grad = rounded(gate_mix[:, 0:1] * back_grad)
    shared_grad = lax.psum_scatter(
        (gate_mix[:, 1:].T[:, :, None] * back_grad[None]).astype(jnp.bfloat16),
        "task",
        scatter_dimension=0,
        tiled=True,
    ).astype(jnp.float32)[0]
    score_grad = gate_mix * (gate_grad - jnp.sum(gate_mix * gate_grad, axis=1, keepdims=True))
    spec_inner = (spec_grad * swish_slope(spec_input)).astype(jnp.bfloat16)
    shared_inner = (shared_grad * swish_slope(shared_input)).astype(jnp.bfloat16)
    field_parts = lax.dot_general(
        spec_inner, spec_full, contract_last, preferred_element_type=jnp.float32
    )
    field_parts = field_parts + lax.dot_general(
        shared_inner, shared_full, contract_last, preferred_element_type=jnp.float32
    )
    field_parts = field_parts + lax.dot_general(
        score_grad,
        gate_own.astype(jnp.float32),
        contract_last,
        precision=highest,
        preferred_element_type=jnp.float32,
    )
    field_grad = lax.psum_scatter(
        field_parts.astype(jnp.bfloat16), "task", scatter_dimension=1, tiled=True
    ).astype(jnp.float32)
    lookup_grad = (field_grad / bag_count[:, None]).astype(jnp.bfloat16)
    per_lookup = jnp.where(live_slot[:, None], lookup_grad[sample_of], jnp.zeros((), jnp.bfloat16))
    outgoing = (
        jnp.zeros((owners * capacity, emb_width), jnp.bfloat16).at[slot_index].set(per_lookup)
    )
    incoming = lax.all_to_all(
        outgoing.reshape(owners, capacity, emb_width),
        ("table", "fsdp"),
        split_axis=0,
        concat_axis=0,
        tiled=True,
    )
    slot_grads = incoming.reshape(owners * capacity, emb_width)
    table_grad = jax.ops.segment_sum(
        slot_grads.astype(jnp.float32),
        mapped_rows.reshape(owners * capacity),
        num_segments=rows_dev,
    )
    return (logit_own[:, None], table_grad[None])


def solution(mesh):
    return jax.shard_map(
        local,
        mesh=mesh,
        in_specs=(
            P(("table", "fsdp"), "task", None),
            P(("table", "fsdp"), "task"),
            P(("table", "fsdp"), "task"),
            P("task", ("table", "fsdp"), None),
            P("task", ("table", "fsdp")),
            P("task", "fsdp", None),
            P("task", "fsdp", None),
            P(),
            P("task", "fsdp", None),
            P("task", None),
        ),
        out_specs=(P(("table", "fsdp"), "task"), P("task", ("table", "fsdp"), None)),
        check_vma=False,
    )
```

profile of v0, /device:TPU:3, one launch (start us, length us, event | category | flops | bytes accessed | tf_op | source)
XLA Modules:
  0.0 713.2 jit_solution(13347347881139238370)
XLA Ops:
  7.9 0.8 copy.27
  8.9 0.8 iota_compare_fusion.2
  10.0 18.4 %reduce-window.6 = s32[64,32,128]{2,1,0:T(8,128)S(1)} reduce-window(s32[64,32,128]{2,1,0:T(8,128)S(1)} %fusion.30, s32[]{:T(128)} %constant.63.clone.1), window={size=1x1x128 pad=0_0x0_0x127_0}, to_apply=%region_0.1 | reduce-window | flops 33292288 | bytes 2097156 | tf_op jit(solution)/shard_map/reduce-window
  29.9 0.8 fusion.26
  30.8 15.5 %scatter_custom_fusion = s32[12288]{0:T(1024)S(1)} fusion(s32[4096]{0:T(1024)S(1)} %bitcast.118, s32[4096]{0:T(1024)S(1)} %get-tuple-element.6, s32[]{:T(128)} %constant.36.clone.1), kind=kCustom, calls=%fused_computation.86 | custom fusion | bytes 49156 | tf_op jit(solution)/shard_map/scatter | solution.py:59
  46.5 21.0 %all_to_all.19 = s32[64,1,192]{2,1,0:T(1,128)S(1)} all-to-all(s32[64,1,192]{2,1,0:T(1,128)S(1)} %all_to_all.12), channel_id=1, replica_groups=mesh['table'=32,'task'=4,'fsdp'=2] {'table','fsdp'}, dimensions={0} | all-to-all | bytes 98304 | tf_op jit(solution)/shard_map/all_to_all | solution.py:65
  67.7 68.0 %gather_fusion = s32[12288]{0:T(1024)S(1)} fusion(s32[8192]{0:T(1024)S(1)} %bitcast.106, s32[12288]{0:T(1024)S(1)} %broadcast_clamp_fusion.1), kind=kCustom, calls=%fused_computation | custom fusion | bytes 147456 | tf_op jit(solution)/shard_map/gather | solution.py:67
  135.9 43.3 %gather_fusion.1 = bf16[12288,128]{1,0:T(8,128)(2,1)} fusion(bf16[4096,128]{1,0:T(8,128)(2,1)S(1)} %bitcast.105, s32[12288]{0:T(1024)S(1)} %broadcast_clamp_fusion), kind=kCustom, calls=%fused_computation.1 | custom fusion | bytes 6340608 | tf_op jit(solution)/shard_map/gather | solution.py:68
  179.2 7.0 broadcast_select_fusion
  186.2 5.8 all-to-all-start.1
  192.8 2.3 copy.35
  195.2 68.6 %all-to-all-done.1 = bf16[64,192,128]{2,1,0:T(8,128)(2,1)S(1)} async-done(((bf16[64,192,128]{2,1,0:T(8,128)(2,1)}), bf16[64,192,128]{2,1,0:T(8,128)(2,1)S(1)}, u32[]{:S(2)}, u32[]{:S(2)}) %all-to-all-start.1) | async-done | bytes 3145760 | tf_op jit(solution)/shard_map/all_to_all | solution.py:69
  263.8 15.0 %gather_fusion.2 = bf16[4096,128]{1,0:T(8,128)(2,1)} fusion(bf16[12288,128]{1,0:T(8,128)(2,1)S(1)} %bitcast.107, s32[4096]{0:T(1024)S(1)} %broadcast_clamp_fusion.3), kind=kCustom, calls=%fused_computation.2 | custom fusion | bytes 2113536 | tf_op jit(solution)/shard_map/gather | solution.py:72
  278.8 3.0 fusion.11
  281.9 9.3 %all_gather.15 = bf16[256,512]{1,0:T(8,128)(2,1)S(1)} all-gather(bf16[256,128]{1,0:T(8,128)(2,1)S(1)} %divide_convert_fusion.1), channel_id=1, replica_groups=mesh['table'=32,'task'=4,'fsdp'=2] {'task'}, dimensions={1}, use_global_device_ids=true | all-gather | bytes 327680 | tf_op jit(solution)/shard_map/all_gather | solution.py:76
  291.3 6.2 multiply_convert_fusion.3
  298.1 5.4 fusion.9
  303.5 80.1 %all-gather.15.cloned.1.call-done = bf16[1024,4096]{1,0:T(8,128)(2,1)} async-done(((bf16[256,4096]{1,0:T(8,128)(2,1)}), bf16[1024,4096]{1,0:T(8,128)(2,1)}) %all-gather.15.cloned.1.call-update) | async-done | bytes 8388624 | tf_op jit(solution)/shard_map/all_gather | solution.py:91
  383.6 6.5 multiply_reduce_fusion.1
  390.1 1.5 multiply_reduce_fusion.3
  391.8 0.8 multiply_convert_fusion.2
  392.6 5.7 multiply_convert_fusion
  398.8 83.9 %reduce-scatter.5.cloned.1.call-done = bf16[1,256,4096]{2,1,0:T(8,128)(2,1)} async-done(((bf16[4,256,4096]{2,1,0:T(8,128)(2,1)}), bf16[1,256,4096]{2,1,0:T(8,128)(2,1)}) %reduce-scatter.5.cloned.1.call-update) | async-done | bytes 2097168 | tf_op jit(solution)/shard_map/reduce_scatter | solution.py:116
  482.6 6.0 fusion.3
  489.1 2.0 fusion.21
  491.6 0.8 copy.37
  492.6 20.7 %reduce-scatter.7.cloned.1.call-done = bf16[128,256]{1,0:T(8,128)(2,1)} async-done(((bf16[512,256]{1,0:T(8,128)(2,1)}), bf16[128,256]{1,0:T(8,128)(2,1)}) %reduce-scatter.7.cloned.1.call-update) | async-done | bytes 65552
  513.3 0.9 copy.38
  514.4 27.6 %scatter_custom_fusion.1 = bf16[12288,128]{1,0:T(8,128)(2,1)} fusion(s32[4096]{0:T(1024)S(1)} %bitcast.120, bf16[]{:T(256)} %constant.70.clone.1, pred[4096]{0:T(1024)(128)(4,1)S(1)} %lt.66, bf16[256,128]{1,0:T(8,128)(2,1)S(1)} %divide_convert_fusion, s32[4096]{0:T(1024)S(1)} %broadcast_clamp_fusion.2), kind=kCustom, calls=%fused_computation.35 | custom fusion | flops 524288 | bytes 3232768 | tf_op jit(solution)/shard_map/scatter | solution.py:144
  542.0 13.2 %all-to-all-start.2 = ((bf16[64,192,128]{2,1,0:T(8,128)(2,1)}), bf16[64,192,128]{2,1,0:T(8,128)(2,1)}, u32[]{:S(2)}, u32[]{:S(2)}) async-start(bf16[64,192,128]{2,1,0:T(8,128)(2,1)} %bitcast.109), calls=%async_computation.3 | async-start | bytes 6291456 | tf_op jit(solution)/shard_map/all_to_all | solution.py:146
  555.5 71.5 %all-to-all-done.2 = bf16[64,192,128]{2,1,0:T(8,128)(2,1)} async-done(((bf16[64,192,128]{2,1,0:T(8,128)(2,1)}), bf16[64,192,128]{2,1,0:T(8,128)(2,1)}, u32[]{:S(2)}, u32[]{:S(2)}) %all-to-all-start.2) | async-done | bytes 3145760 | tf_op jit(solution)/shard_map/all_to_all | solution.py:146
  627.0 79.4 %scatter_custom_fusion.2 = f32[4096,128]{1,0:T(8,128)} fusion(s32[12288]{0:T(1024)S(1)} %bitcast.123, bf16[12288,128]{1,0:T(8,128)(2,1)} %bitcast.38, f32[]{:T(128)} %constant.71.clone.1), kind=kCustom, calls=%fused_computation.8 | custom fusion | flops 3145728 | bytes 5242884 | tf_op jit(solution)/shard_map/scatter-add | solution.py:154
  (79 shorter events, 6.5 us)
Async XLA Ops:
  7.2 128.8 %copy-start = (bf16[1,4096,128]{2,1,0:T(8,128)(2,1)S(1)}, bf16[1,4096,128]{2,1,0:T(8,128)(2,1)}, u32[]{:S(2)}) copy-start(bf16[1,4096,128]{2,1,0:T(8,128)(2,1)} %param.13) | copy-start | bytes 3145732
  7.2 284.1 %all-gather.13.cloned.1.call-start = ((), (), s32[]{:S(2)}) async-start(), calls=%async_computation.8 | async-start | bytes 6291456 | tf_op jit(solution)/shard_map/all_gather | solution.py:82
  28.4 39.2 %copy-start.2 = (s32[1,8192]{1,0:T(1,128)S(1)}, s32[1,8192]{1,0:T(1,128)}, u32[]{:S(2)}) copy-start(s32[1,8192]{1,0:T(1,128)} %param.14) | copy-start | bytes 98308
  186.2 77.6 %all-to-all-start.1 = ((bf16[64,192,128]{2,1,0:T(8,128)(2,1)}), bf16[64,192,128]{2,1,0:T(8,128)(2,1)S(1)}, u32[]{:S(2)}, u32[]{:S(2)}) async-start(bf16[64,192,128]{2,1,0:T(8,128)(2,1)} %broadcast_select_fusion), calls=%async_computation.1 | async-start | bytes 6291456 | tf_op jit(solution)/shard_map/all_to_all | solution.py:69
  191.9 3.2 copy-start.8
  192.0 106.1 %all-gather.9.cloned.1.call-start = ((), (), s32[]{:S(2)}) async-start(), calls=%async_computation.6 | async-start | bytes 6291456 | tf_op jit(solution)/shard_map/all_gather | solution.py:81
  192.7 110.8 %all-gather.11.cloned.1.call-start = ((), (), s32[]{:S(2)}) async-start(), calls=%async_computation.7 | async-start | bytes 3145728 | tf_op jit(solution)/shard_map/all_gather | solution.py:83
  195.1 188.5 %all-gather.15.cloned.1.call-start = ((), (), s32[]{:S(2)}) async-start(), calls=%async_computation.9 | async-start | bytes 10485760 | tf_op jit(solution)/shard_map/all_gather | solution.py:91
  291.3 6.5 copy-start.11
  291.3 6.5 copy-start.7
  297.5 185.1 %reduce-scatter.5.cloned.1.call-start = ((), (), s32[]{:S(2)}) async-start(), calls=%async_computation.5 | async-start | bytes 10485760 | tf_op jit(solution)/shard_map/reduce_scatter | solution.py:116
  383.6 6.5 copy-start.4
  383.6 6.5 copy-start.6
  390.1 1.5 copy-start.9
  391.6 1.0 copy-start.10
  398.4 114.9 %reduce-scatter.7.cloned.1.call-start = ((), (), s32[]{:S(2)}) async-start(), calls=%async_computation.10 | async-start | bytes 327680
  482.6 6.0 copy-start.3
  482.6 6.5 copy-start.5
  542.0 85.0 %all-to-all-start.2 = ((bf16[64,192,128]{2,1,0:T(8,128)(2,1)}), bf16[64,192,128]{2,1,0:T(8,128)(2,1)}, u32[]{:S(2)}, u32[]{:S(2)}) async-start(bf16[64,192,128]{2,1,0:T(8,128)(2,1)} %bitcast.109), calls=%async_computation.3 | async-start | bytes 6291456 | tf_op jit(solution)/shard_map/all_to_all | solution.py:146
  555.3 151.1 %copy-start.1 = (bf16[1,4096,128]{2,1,0:T(8,128)(2,1)S(1)}, bf16[1,4096,128]{2,1,0:T(8,128)(2,1)}, u32[]{:S(2)}) copy-start(bf16[1,4096,128]{2,1,0:T(8,128)(2,1)} %param.13) | copy-start | bytes 3145732
Sparse Core Ops, SparseCore 0:
  9.8 22.4 all-gather.12
  194.6 20.4 all-gather.8
  216.9 17.1 all-gather.10
  297.7 85.8 all-gather.14
  398.5 84.1 reduce-scatter.4
  492.6 20.6 reduce-scatter.6
where the time goes:
time: 716 us; the launch traced here: 713 us
  waiting for transfers between devices  326 us (46%)
  local copies, waits for them, and re-layouts  149 us (21%)
  other arithmetic  144 us (20%)
  blocking collectives  30.4 us (4%)
  matrix products  29.1 us (4%)
  starting transfers between devices  19.6 us (3%)
  between operations  14.6 us (2%)
    reduce_scatter x1, waiting for transfers between devices, local(): lax.psum_scatter((gate_mix[:, 1:].T[:, :, None] * back_grad[None]).astype...  83.9 us
    all_gather x1, waiting for transfers between devices, local(): shared_all = lax.all_gather(shared_out[None], 'task', axis=0, tiled=True)  80.1 us
    scatter-add x1, other arithmetic, local(): jax.ops.segment_sum(slot_grads.astype(jnp.float32), mapped_rows.reshape(o...  79.4 us
    all_to_all x1, waiting for transfers between devices, local(): lax.all_to_all(outgoing.reshape(owners, capacity, emb_width), ('table', '...  71.5 us
    all_to_all x1, waiting for transfers between devices, local(): lax.all_to_all(fetched, ('table', 'fsdp'), split_axis=0, concat_axis=0, t...  68.6 us
    gather x2, local copies, waits for them, and re-layouts, local(): mapped_rows = jnp.where(known, row_map[jnp.maximum(asked, 0)], 0)  68.1 us
    gather x1, local copies, waits for them, and re-layouts, local(): shard_rows[mapped_rows]  43.3 us
    scatter x1, other arithmetic, local(): jnp.zeros((owners * capacity, emb_width), jnp.bfloat16).at[slot_index]  27.6 us
  transfers between devices with their start and end apart: 8, of which 5 were waited for; matrix products, arithmetic and copies ran while one was open for 27% of the time, Pallas kernels for 0%

commit v1 on v0

v1 whole, which is shorter than its diff:
```python
import functools

import jax
import jax.numpy as jnp
from jax import lax
from jax.experimental import pallas as pl
from jax.experimental.pallas import tpu as pltpu
from jax.sharding import PartitionSpec as P

loss_scale = 1024.0
highest = lax.Precision.HIGHEST
contract_last = (((1,), (1,)), ((), ()))
bf16 = jnp.bfloat16
f32 = jnp.float32
i32 = jnp.int32
OWNERS = 64
CAP = 64
HOT_CAP = 192
HOT_LANES = 256
RAW_BITS = 13
PIECE_ROWS = 528
VMEM = pl.BlockSpec(memory_space=pltpu.VMEM)
SMEM = pl.BlockSpec(memory_space=pltpu.SMEM)


def params(mib):
    return pltpu.CompilerParams(vmem_limit_bytes=mib * 1024 * 1024)


def iota(shape, dim):
    return lax.broadcasted_iota(i32, shape, dim)


def dot(left, right):
    return jnp.dot(left, right, preferred_element_type=f32)


def dot_last(left, right):
    return lax.dot_general(left, right, contract_last, preferred_element_type=f32)


def one_hot(mask):
    return jnp.where(mask, 1.0, 0.0).astype(bf16)


def bucket_kernel(ids_ref, len_ref, req_ref, hot_ref):
    slots, samples = ids_ref.shape
    owner_row = iota((OWNERS, samples), 0)
    sample1 = (iota((1, samples), 1) + 1).astype(f32)
    before = one_hot(iota((samples, samples), 0) < iota((samples, samples), 1))
    rank_row = iota((HOT_CAP, samples), 0)
    lens = len_ref[...]
    base = jnp.zeros((OWNERS, 1), f32)
    total = jnp.zeros((3 * OWNERS, HOT_CAP), f32)
    for slot in range(slots):
        ids = ids_ref[slot : slot + 1, :]
        owner = jnp.where(lens > slot, ids >> RAW_BITS, -1)
        hit = owner_row == owner
        hit_f = jnp.where(hit, 1.0, 0.0)
        seen = dot(hit_f.astype(bf16), before) + base
        base = base + jnp.sum(hit_f, axis=1, keepdims=True)
        rank = jnp.sum(hit_f * seen, axis=0, keepdims=True).astype(i32)
        raw = ids & ((1 << RAW_BITS) - 1)
        planes = jnp.concatenate(
            [
                hit_f * (raw >> 7).astype(f32),
                hit_f * (raw & 127).astype(f32),
                hit_f * sample1,
            ],
            axis=0,
        ).astype(bf16)
        total = total + dot_last(planes, one_hot(rank_row == rank))
    hot = base > float(CAP)
    high, low, samp = total[:OWNERS], total[OWNERS : 2 * OWNERS], total[2 * OWNERS :]
    cold = jnp.where(hot, 0.0, 1.0)
    warm = 1.0 - cold
    raw_all = high * 128.0 + low
    req_ref[...] = ((samp * cold)[:, :CAP].astype(i32) << 16) + (raw_all * cold)[:, :CAP].astype(
        i32
    )
    hot_samp = jnp.sum(samp * warm, axis=0, keepdims=True).astype(i32)
    hot_raw = jnp.sum(raw_all * warm, axis=0, keepdims=True).astype(i32)
    index = jnp.sum(warm * iota((OWNERS, 1), 0).astype(f32), axis=0, keepdims=True)
    pad = jnp.broadcast_to(index.astype(i32), (1, HOT_LANES - HOT_CAP))
    hot_ref[...] = jnp.concatenate([(hot_samp << 16) + hot_raw, pad], axis=1)


def map_rows(code, map_t):
    lanes = code.shape[1]
    raw = code & 0xFFFF
    spread = one_hot(iota((64, lanes), 0) == (raw >> 7))
    both = dot(map_t, spread)
    wide = both[:128] * 64.0 + both[128:]
    return jnp.sum(
        jnp.where(iota((128, lanes), 0) == (raw & 127), wide, 0.0), axis=0, keepdims=True
    )


def as_column(row):
    return jnp.broadcast_to(row, (128, row.shape[1])).T


def low_one_hot(low):
    lane = iota(low.shape, 1)
    return jnp.concatenate([one_hot(low == lane), one_hot(low == lane + 128)], axis=1)


def pick_rows(spread, high, table_pair, pairs):
    found = jnp.zeros((spread.shape[0], 128), f32)
    for pair in range(pairs):
        both = dot(spread, table_pair(pair))
        found = jnp.where(high == 2 * pair, both[:, :128], found)
        found = jnp.where(high == 2 * pair + 1, both[:, 128:], found)
    return found


def gather_kernel(req_ref, map_ref, table_ref, out_ref, spread_ref, high_ref):
    map_t = map_ref[...]
    chunks = req_ref.shape[0]

    @pl.loop(0, chunks // 4)
    def _(group):
        for part in range(4):
            chunk = group * 4 + part
            code = req_ref[pl.ds(chunk, 1), :]
            row = jnp.where(code >= 65536, map_rows(code, map_t), -1.0)
            column = as_column(row).astype(i32)
            place = pl.ds(pl.multiple_of(chunk * 128, 128), 128)
            spread_ref[place, :] = low_one_hot(column & 255)
            high_ref[place, :] = column >> 8

    block = 512

    @pl.loop(0, out_ref.shape[0] // block)
    def _(step):
        place = pl.ds(pl.multiple_of(step * block, block), block)

        def table_pair(pair):
            return jnp.concatenate(
                [
                    table_ref[pair * 512 : pair * 512 + 256, :],
                    table_ref[pair * 512 + 256 : pair * 512 + 512, :],
                ],
                axis=1,
            )

        out_ref[place, :] = pick_rows(
            spread_ref[place, :], high_ref[place, :], table_pair, 8
        ).astype(bf16)


def map_kernel(code_ref, map_ref, row_ref, samp_ref):
    map_t = map_ref[...]

    @pl.loop(0, code_ref.shape[0] // 4)
    def _(group):
        for part in range(4):
            place = pl.ds(group * 4 + part, 1)
            code = code_ref[place, :]
            row_ref[place, :] = map_rows(code, map_t).astype(i32)
            samp_ref[place, :] = (code >> 16) - 1


def pool_kernel(place_ref, req_ref, hot_ref, rows_ref, own_ref, sib_ref, len_ref, out_ref):
    samples = out_ref.shape[0]
    sample_col = iota((samples, 128), 0)
    summed = jnp.zeros((samples, 128), f32)
    for pair in range(req_ref.shape[0] // 2):
        parts = [
            one_hot(sample_col == (req_ref[2 * pair + half : 2 * pair + half + 1, :] >> 16) - 1)
            for half in range(2)
        ]
        summed = summed + dot(
            jnp.concatenate(parts, axis=1), rows_ref[pair * 256 : pair * 256 + 256, :]
        )
    across, core = place_ref[1], place_ref[2]

    def piece(index, start, size):
        half, slot = index // 4, (across - index % 4) & 3
        own = own_ref[slot, start : start + size, :].astype(f32)
        sib = sib_ref[slot, start : start + size, :].astype(f32)
        return jnp.where(core == half, own, sib)

    planes = [
        jnp.concatenate([piece(4 * plane + part, 512, 16) for part in range(4)], axis=0).T
        for plane in range(2)
    ]
    map_t = jnp.concatenate(planes, axis=0).astype(bf16)
    code = jnp.where(iota((1, HOT_LANES), 1) < HOT_CAP, hot_ref[...], 0)
    row = jnp.where(code >= 65536, map_rows(code, map_t), -1.0)
    column = as_column(row).astype(i32)

    def table_pair(pair):
        return jnp.concatenate(
            [piece(pair, 0, 256), piece(pair, 256, 256)], axis=1
        ).astype(bf16)

    hot_rows = pick_rows(low_one_hot(column & 255), column >> 8, table_pair, 8).astype(bf16)
    spread = one_hot(iota((samples, HOT_LANES), 0) == (code >> 16) - 1)
    summed = summed + dot(spread, hot_rows)
    out_ref[...] = (summed / len_ref[...].astype(f32)).astype(bf16)


def scatter_kernel(steps, place_ref, row_ref, samp_ref, *refs):
    count = len(steps)
    grads = refs[: 2 * count]
    if len(refs) == 2 * count + 3:
        out_ref, wide_ref, spread_ref = refs[2 * count :]
        out_ref[...] = jnp.zeros_like(out_ref)
    else:
        seen_ref, out_ref, wide_ref, spread_ref = refs[2 * count :]
        out_ref[...] = seen_ref[...]
    depth, across, core, chunks = place_ref[0], place_ref[1], place_ref[2], place_ref[3]
    lane = iota((1, 128), 1)
    offset = jnp.where(lane < 64, core * 256, (1 - core) * 256)
    lane_wide = iota((128, 128), 1)
    low_row = iota((256, 128), 0)
    for index, step in enumerate(steps):
        own_ref, sib_ref = grads[2 * index], grads[2 * index + 1]
        level = ((depth - step) & 7) * 4

        @pl.loop(0, chunks)
        def _(chunk):
            for shift in range(4):
                block = level + ((across - shift) & 3)
                row = row_ref[block, pl.ds(chunk, 1), :]
                samp = samp_ref[block, pl.ds(chunk, 1), :]
                samp = jnp.where(samp < 0, -1, samp + offset)
                samp_col = as_column(samp.astype(f32)).astype(i32)
                high_col = as_column((row >> 8).astype(f32)).astype(i32)
                picks = jnp.concatenate(
                    [one_hot(samp_col == lane_wide + 128 * part) for part in range(4)], axis=1
                )
                source = jnp.concatenate([own_ref[shift], sib_ref[shift]], axis=0)
                slots = dot(picks, source)
                place = slice(shift * 128, shift * 128 + 128)
                for high in range(16):
                    wide_ref[place, high * 128 : high * 128 + 128] = jnp.where(
                        high_col == high, slots, 0.0
                    ).astype(bf16)
                spread_ref[:, place] = one_hot(low_row == (row & 255))
            spread = spread_ref[...]
            for pair in range(8):
                both = dot(spread, wide_ref[:, pair * 256 : pair * 256 + 256])
                start = pair * 512
                out_ref[start : start + 256, :] += both[:, :128]
                out_ref[start + 256 : start + 512, :] += both[:, 128:]


def scatter_call(steps, place, rows, samps, grads, seen):
    operands = [place, rows, samps, *grads]
    aliases = {}
    if seen is not None:
        operands.append(seen)
        aliases = {len(operands) - 1: 0}
    return pl.pallas_call(
        functools.partial(scatter_kernel, steps),
        out_shape=jax.ShapeDtypeStruct((4096, 128), f32),
        in_specs=[SMEM] + [VMEM] * (len(operands) - 1),
        out_specs=VMEM,
        scratch_shapes=[pltpu.VMEM((512, 2048), bf16), pltpu.VMEM((256, 512), bf16)],
        input_output_aliases=aliases,
        compiler_params=params(32),
    )(*operands)


def swish_slope(value):
    sigmoid_val = jax.nn.sigmoid(value)
    return sigmoid_val * (1.0 + value * (1.0 - sigmoid_val))


def ring(size, shift):
    return [(i, (i + shift) % size) for i in range(size)]


def along_task(value, shift):
    return lax.ppermute(value, "task", ring(4, shift))


def across_core(value):
    return lax.ppermute(value, "fsdp", [(0, 1), (1, 0)])


def along_x(value, shift):
    return lax.ppermute(
        value, "table", [(z * 4 + x, z * 4 + (x + shift) % 4) for z in range(8) for x in range(4)]
    )


def along_z(value, shift):
    return lax.ppermute(
        value,
        "table",
        [(z * 4 + x, (z + shift) % 8 * 4 + x) for z in range(8) for x in range(4)],
    )


def at(stack, index):
    return lax.dynamic_index_in_dim(stack, index, 0, keepdims=False)


def local(
    raw_ids,
    bag_len,
    labels,
    emb_table,
    bucket_map,
    spec_weight,
    shared_weight,
    gate_weight,
    tower_weight,
    head_vector,
):
    task = lax.axis_index("task")
    core = lax.axis_index("fsdp")
    table_index = lax.axis_index("table")
    depth, across = table_index // 4, table_index % 4
    me = table_index * 2 + core
    samples = raw_ids.shape[0]
    lookups = OWNERS * CAP

    tower_all = lax.all_gather(tower_weight[0], ("task", "fsdp"), axis=0, tiled=True)
    tower_all = tower_all.reshape(4, 4096, 256)
    spec_sib = across_core(spec_weight[0])
    shared_sib = across_core(shared_weight[0])

    def joined(own, sib):
        return jnp.concatenate(
            [jnp.where(core == 0, own, sib), jnp.where(core == 0, sib, own)], axis=0
        )

    ids_t = raw_ids[:, 0, :].T
    req, hot_row = pl.pallas_call(
        bucket_kernel,
        out_shape=(
            jax.ShapeDtypeStruct((OWNERS, CAP), i32),
            jax.ShapeDtypeStruct((1, HOT_LANES), i32),
        ),
        in_specs=[VMEM] * 2,
        out_specs=(VMEM, VMEM),
        compiler_params=params(16),
    )(ids_t, bag_len.reshape(1, samples))
    hot_index = hot_row[0, HOT_CAP]
    hot_z, hot_x, hot_c = hot_index // 8, hot_index // 2 % 4, hot_index % 2
    away_z, away_x = (depth - hot_z) % 8, (across - hot_x) % 4

    row_map = bucket_map[0].reshape(64, 128)
    planes = jnp.concatenate([row_map >> 6, row_map & 63], axis=0).astype(bf16)
    map_t = jnp.concatenate([(row_map >> 6).T, (row_map & 63).T], axis=0).astype(bf16)
    shard_rows = emb_table[0]

    pieces = jnp.concatenate(
        [shard_rows.reshape(8, 512, 128), planes.reshape(8, 16, 128)], axis=1
    ).reshape(2, 4, PIECE_ROWS, 128)
    half = jnp.where(hot_c == core, at(pieces, core), across_core(at(pieces, 1 - core)))

    asked = lax.all_to_all(req, ("table", "fsdp"), split_axis=0, concat_axis=0, tiled=True)
    asked = asked.reshape(lookups // 128, 128)

    quarters = [at(half, across)] + [
        along_x(at(half, (across + shift) % 4), shift) for shift in (1, 2, 3)
    ]
    part = lax.select_n(away_x, *quarters)
    part = lax.select_n(
        jnp.where(away_z == 1, 1, jnp.where(away_z == 7, 2, 0)),
        part,
        along_z(part, 1),
        along_z(part, 7),
    )
    part = lax.select_n(
        jnp.where((away_z >= 2) & (away_z <= 4), 1, jnp.where((away_z == 5) | (away_z == 6), 2, 0)),
        part,
        along_z(part, 3),
        along_z(part, 5),
    )
    hot_own = jnp.stack([part] + [along_x(part, shift) for shift in (1, 2, 3)])
    hot_sib = across_core(hot_own)

    fetched = pl.pallas_call(
        gather_kernel,
        out_shape=jax.ShapeDtypeStruct((lookups, 128), bf16),
        in_specs=[VMEM] * 3,
        out_specs=VMEM,
        scratch_shapes=[pltpu.VMEM((lookups, 256), bf16), pltpu.VMEM((lookups, 128), i32)],
        compiler_params=params(32),
    )(asked, map_t, shard_rows)
    returned = lax.all_to_all(
        fetched.reshape(OWNERS, CAP, 128),
        ("table", "fsdp"),
        split_axis=0,
        concat_axis=0,
        tiled=True,
    ).reshape(lookups, 128)

    place = jnp.stack([depth, across, core]).astype(i32)
    pooled = pl.pallas_call(
        pool_kernel,
        out_shape=jax.ShapeDtypeStruct((samples, 128), bf16),
        in_specs=[SMEM] + [VMEM] * 6,
        out_specs=VMEM,
        compiler_params=params(32),
    )(place, req.reshape(lookups // 128, 128), hot_row, returned, hot_own, hot_sib, bag_len)

    hot_all = lax.all_gather(hot_row[0, :HOT_CAP], ("table", "fsdp"), axis=0, tiled=False)
    is_hot = hot_index == me
    hot_codes = hot_all.reshape(32, 2, 3, 64).transpose(0, 2, 1, 3).reshape(32, 3, 128)
    cold_codes = jnp.pad(asked[:, None, :], ((0, 0), (0, 2), (0, 0)))
    codes = jnp.where(is_hot, hot_codes, cold_codes).reshape(96, 128)
    rows, samps = pl.pallas_call(
        map_kernel,
        out_shape=(jax.ShapeDtypeStruct((96, 128), i32),) * 2,
        in_specs=[VMEM] * 2,
        out_specs=(VMEM, VMEM),
        compiler_params=params(16),
    )(codes, map_t)
    rows, samps = rows.reshape(32, 3, 128), samps.reshape(32, 3, 128)

    felt = jnp.stack([pooled] + [along_task(pooled, shift) for shift in (1, 2, 3)])
    features = jnp.concatenate([at(felt, (task - field) % 4) for field in range(4)], axis=1)
    spec_full = joined(spec_weight[0], spec_sib)
    shared_full = joined(shared_weight[0], shared_sib)
    tower_own = at(tower_all, task)
    targets = labels[:, 0].astype(f32)
    head_row = head_vector[0].astype(f32)

    spec_input = dot(features, spec_full)
    shared_input = dot(features, shared_full)
    spec_out = jax.nn.silu(spec_input).astype(bf16)
    shared_out = jax.nn.silu(shared_input).astype(bf16)
    scores = jnp.einsum("si,tig->tsg", features, gate_weight, preferred_element_type=f32)
    raised = jnp.exp(scores)
    gate_mix = raised / jnp.sum(raised, axis=-1, keepdims=True)
    mix_shared = lax.dynamic_index_in_dim(gate_mix, task + 1, 2, keepdims=True)
    mix_own = at(gate_mix, task)
    spec_proj = dot(spec_out, tower_own)
    shared_proj = jnp.einsum("sd,tdh->tsh", shared_out, tower_all, preferred_element_type=f32)
    partial = mix_shared * shared_proj
    own_partial = at(partial, task) + mix_own[:, 0:1] * spec_proj
    sent = partial.astype(bf16)
    tower_pre = own_partial
    for shift in (1, 2, 3):
        tower_pre = tower_pre + along_task(at(sent, (task + shift) % 4), shift).astype(f32)
    logit_own = jnp.sum(jax.nn.silu(tower_pre) * head_row[None, :], axis=1)
    logit_grad = loss_scale * (jax.nn.sigmoid(logit_own) - targets)
    pre_grad = (logit_grad[:, None] * head_row[None, :] * swish_slope(tower_pre)).astype(bf16)
    pre_rel = jnp.stack([pre_grad] + [along_task(pre_grad, shift) for shift in (1, 2, 3)])
    pre_all = jnp.stack([at(pre_rel, (task - other) % 4) for other in range(4)])
    pre_wide = pre_grad.astype(f32)
    balance = jnp.sum(pre_wide * tower_pre, axis=1, keepdims=True)
    shared_score = mix_shared[:, :, 0].T * jnp.sum(pre_all.astype(f32) * shared_proj, axis=2).T
    spec_score = mix_own[:, 0:1] * jnp.sum(pre_wide * spec_proj, axis=1, keepdims=True)
    spec_grad = dot_last((mix_own[:, 0:1] * pre_wide).astype(bf16), tower_own)
    weighted = (mix_shared * pre_all.astype(f32)).astype(bf16)
    shared_grad = jnp.einsum("tsh,tdh->sd", weighted, tower_all, preferred_element_type=f32)
    spec_inner = (spec_grad * swish_slope(spec_input)).astype(bf16)
    shared_inner = (shared_grad * swish_slope(shared_input)).astype(bf16)
    gate_f = gate_weight.astype(f32)
    gate_own = at(gate_f, task)
    gate_shared = lax.dynamic_index_in_dim(gate_f, task + 1, 2, keepdims=False)
    score_grad = jnp.concatenate(
        [shared_score, spec_score, -mix_own * balance], axis=1
    )
    score_weight = jnp.concatenate([gate_shared, gate_own[:, 0:1].T, gate_own.T], axis=0)
    field_parts = (
        dot_last(spec_inner, spec_full)
        + dot_last(shared_inner, shared_full)
        + jnp.dot(score_grad, score_weight, precision=highest, preferred_element_type=f32)
    )
    blocks = field_parts.reshape(samples, 4, 128)
    blocks = jnp.moveaxis(blocks, 1, 0)
    field_grad = at(blocks, task)
    sent_blocks = blocks.astype(bf16)
    for shift in (1, 2, 3):
        field_grad = field_grad + along_task(at(sent_blocks, (task + shift) % 4), shift).astype(f32)
    lookup_grad = (field_grad / bag_len.astype(f32)).astype(bf16)

    place4 = jnp.stack([depth, across, core, jnp.where(is_hot, 3, 1)]).astype(i32)
    near = jnp.stack([lookup_grad] + [along_x(lookup_grad, shift) for shift in (1, 2, 3)])
    near_sib = across_core(near)
    table_grad = scatter_call((0,), place4, rows, samps, [near, near_sib], None)
    up, down = near, near
    for step in (1, 2, 3):
        up, down = along_z(up, 1), along_z(down, 7)
        up_sib, down_sib = across_core(up), across_core(down)
        table_grad = scatter_call(
            (step, -step), place4, rows, samps, [up, up_sib, down, down_sib], table_grad
        )
    far = jnp.concatenate([along_z(up[:2], 1), along_z(down[2:], 7)], axis=0)
    far_sib = across_core(far)
    table_grad = scatter_call((4,), place4, rows, samps, [far, far_sib], table_grad)
    return (logit_own[:, None], table_grad[None])


def solution(mesh):
    return jax.shard_map(
        local,
        mesh=mesh,
        in_specs=(
            P(("table", "fsdp"), "task", None),
            P(("table", "fsdp"), "task"),
            P(("table", "fsdp"), "task"),
            P("task", ("table", "fsdp"), None),
            P("task", ("table", "fsdp")),
            P("task", "fsdp", None),
            P("task", "fsdp", None),
            P(),
            P("task", "fsdp", None),
            P("task", None),
        ),
        out_specs=(P(("table", "fsdp"), "task"), P("task", ("table", "fsdp"), None)),
        check_vma=False,
    )
```

time: 716 us -> 348 us (0.49)
  waiting for transfers between devices: 326 us -> 55.2 us
  local copies, waits for them, and re-layouts: 149 us -> 10.5 us
  other arithmetic: 144 us -> 13.2 us
  starting transfers between devices: 19.6 us -> 101 us
  Pallas kernels: 0 us -> 66.5 us
  blocking collectives: 30.4 us -> 44.7 us
    all_to_all x2, waiting for transfers between devices: 140 us -> 4.98 us  [the longest x1 4.98 us: local(): lax.all_to_all(req, ('table', 'fsdp'), split_axis=0, concat_axis=0, tiled...]
    gather x4 -> x0, local copies, waits for them, and re-layouts: 126 us -> none  [the longest x2 68.1 us: local(): mapped_rows = jnp.where(known, row_map[jnp.maximum(asked, 0)], 0)]
    reduce_scatter x1 -> x0, waiting for transfers between devices: 83.9 us -> none  [local(): lax.psum_scatter((gate_mix[:, 1:].T[:, :, None] * back_grad[None]).astype...]
    ppermute x0 -> x45, starting transfers between devices: none -> 83 us  [the longest x12 25.3 us: along_task(): return lax.ppermute(value, 'task', ring(4, shift))]
    all_gather x4 -> x1, waiting for transfers between devices: 80.1 us -> 0.02 us  [local(): lax.all_gather(tower_weight[0], ('task', 'fsdp'), axis=0, tiled=True)]
    scatter-add x1 -> x0, other arithmetic: 79.4 us -> none  [local(): jax.ops.segment_sum(slot_grads.astype(jnp.float32), mapped_rows.reshape(o...]
    pallas_call x0 -> x9, Pallas kernels: none -> 66.5 us  [the longest x5 47.2 us: scatter_call(): pl.pallas_call(functools.partial(scatter_kernel, steps), out_shape=jax.Sh...]
    ppermute x0 -> x45, waiting for transfers between devices: none -> 49.5 us  [the longest x12 24.6 us: along_z(): lax.ppermute(value, 'table', [(z * 4 + x, (z + shift) % 8 * 4 + x) for z...]
  transfers between devices with their start and end apart: 8 -> 48, of which waited for: 5 -> 20; matrix products, arithmetic and copies ran while one was open for 27% -> 6% of each run, Pallas kernels for 0% -> 17%
where the time goes in v1:
time: 348 us; the launch traced here: 342 us
  starting transfers between devices  101 us (29%)
  Pallas kernels  66.5 us (19%)
  waiting for transfers between devices  55.2 us (16%)
  blocking collectives  44.7 us (13%)
  matrix products  32.6 us (9%)
  between operations  18.3 us (5%)
  other arithmetic  13.2 us (4%)
  local copies, waits for them, and re-layouts  10.5 us (3%)
    pallas_call x5, Pallas kernels, scatter_call(): pl.pallas_call(functools.partial(scatter_kernel, steps), out_shape=jax.Sh...  47.2 us
    all_gather x1, blocking collectives, local(): lax.all_gather(hot_row[0, :HOT_CAP], ('table', 'fsdp'), axis=0, tiled=False)  44.7 us
    ppermute x12, starting transfers between devices, along_task(): return lax.ppermute(value, 'task', ring(4, shift))  25.3 us
    ppermute x12, waiting for transfers between devices, along_z(): lax.ppermute(value, 'table', [(z * 4 + x, (z + shift) % 8 * 4 + x) for z...  24.6 us
    ppermute x12, starting transfers between devices, across_core(): return lax.ppermute(value, 'fsdp', [(0, 1), (1, 0)])  24.1 us
    ppermute x12, starting transfers between devices, along_z(): lax.ppermute(value, 'table', [(z * 4 + x, (z + shift) % 8 * 4 + x) for z...  21.6 us
    dot_general x2, matrix products, dot_last(): lax.dot_general(left, right, contract_last, preferred_element_type=f32)  15.1 us
    ppermute x9, waiting for transfers between devices, along_x(): lax.ppermute(value, 'table', [(z * 4 + x, z * 4 + (x + shift) % 4) for z...  13.8 us
  transfers between devices with their start and end apart: 48, of which 20 were waited for; matrix products, arithmetic and copies ran while one was open for 6% of the time, Pallas kernels for 17%

profile of v1, /device:TPU:3, one launch (start us, length us, event | category | flops | bytes accessed | tf_op | source)
XLA Modules:
  0.0 341.7 jit_solution(18304768491296535002)
XLA Ops:
  14.4 11.8 %all-to-all-start = ((s32[64,1,64]{2,1,0:T(1,128)}), s32[64,1,64]{2,1,0:T(1,128)S(1)}, u32[]{:S(2)}, u32[]{:S(2)}) async-start(s32[64,1,64]{2,1,0:T(1,128)} %bitcast.7), calls=%async_computation | async-start | bytes 65536 | tf_op jit(solution)/shard_map/all_to_all | solution.py:357
  29.5 5.0 %all-to-all-done = s32[64,1,64]{2,1,0:T(1,128)S(1)} async-done(((s32[64,1,64]{2,1,0:T(1,128)}), s32[64,1,64]{2,1,0:T(1,128)S(1)}, u32[]{:S(2)}, u32[]{:S(2)}) %all-to-all-start) | async-done | bytes 16416 | tf_op jit(solution)/shard_map/all_to_all | solution.py:357
  37.1 9.5 %shard_map.114 = bf16[4096,128]{1,0:T(8,128)(2,1)} custom-call(s32[32,128]{1,0:T(8,128)S(1)} %reshape.84.req_ref, bf16[256,64]{1,0:T(8,128)(2,1)S(1)} %pad_maximum_fusion.20.map_ref, bf16[4096,128]{1,0:T(8,128)(2,1)S(1)} %bitcast.177), custom_call_target="tpu_custom_call" | custom-call | tf_op jit(solution)/shard_map/pallas_call | solution.py:379
  46.6 5.9 %all-to-all-start.1 = ((bf16[64,64,128]{2,1,0:T(8,128)(2,1)}), bf16[64,64,128]{2,1,0:T(8,128)(2,1)S(1)}, u32[]{:S(2)}, u32[]{:S(2)}) async-start(bf16[64,64,128]{2,1,0:T(8,128)(2,1)} %bitcast.11), calls=%async_computation.1 | async-start | bytes 2097152 | tf_op jit(solution)/shard_map/all_to_all | solution.py:387
  61.9 3.7 %collective-permute-done.3 = bf16[528,128]{1,0:T(8,128)(2,1)S(1)} collective-permute-done((bf16[528,128]{1,0:T(8,128)(2,1)S(1)}, bf16[528,128]{1,0:T(8,128)(2,1)S(1)}, u32[]{:S(2)}, u32[]{:S(2)}) %collective-permute-start.3) | collective-permute-done | bytes 135200 | tf_op jit(solution)/shard_map/ppermute | solution.py:285
  66.7 3.4 collective-permute-start.5
  70.1 10.9 %collective-permute-done.4 = bf16[528,128]{1,0:T(8,128)(2,1)S(1)} collective-permute-done((bf16[528,128]{1,0:T(8,128)(2,1)S(1)}, bf16[528,128]{1,0:T(8,128)(2,1)S(1)}, u32[]{:S(2)}, u32[]{:S(2)}) %collective-permute-start.4) | collective-permute-done | bytes 135200 | tf_op jit(solution)/shard_map/ppermute | solution.py:291
  81.1 3.2 collective-permute-start.6
  89.1 4.4 %collective-permute-done.6 = bf16[528,128]{1,0:T(8,128)(2,1)S(1)} collective-permute-done((bf16[528,128]{1,0:T(8,128)(2,1)S(1)}, bf16[528,128]{1,0:T(8,128)(2,1)S(1)}, u32[]{:S(2)}, u32[]{:S(2)}) %collective-permute-start.6) | collective-permute-done | bytes 135200 | tf_op jit(solution)/shard_map/ppermute | solution.py:291
  101.4 4.1 %collective-permute-start.11 = (bf16[4,528,128]{2,1,0:T(8,128)(2,1)S(1)}, bf16[4,528,128]{2,1,0:T(8,128)(2,1)S(1)}, u32[]{:S(2)}, u32[]{:S(2)}) collective-permute-start(bf16[4,528,128]{2,1,0:T(8,128)(2,1)S(1)} %pad_maximum_fusion.12.own_ref), channel_id=1, source_target_pairs={{0,1},{1,0},{2,3},{3,2},{4,5},{5,4},{6,7},{7,6},{8,9},{9,8},{10,11... | collective-permute-start | bytes 1622024 | tf_op jit(solution)/shard_map/ppermute | solution.py:281
  114.2 3.8 %broadcast_select_fusion.1 = (bf16[256,4096]{1,0:T(8,128)(2,1)S(1)}, bf16[256,4096]{1,0:T(8,128)(2,1)}) fusion(bf16[256,4096]{1,0:T(8,128)(2,1)} %collective-permute-done.16, pred[]{:T(512)S(6)} %eq.52, bf16[1,256,4096]{2,1,0:T(8,128)(2,1)} %param.15), kind=kLoop, calls=%fused_computation.21 | loop fusion | flops 2097152 | bytes 8388609 | tf_op jit(solution)/shard_map/jit(_where)/select_n | solution.py:329
  122.0 3.2 fusion.6
  125.3 8.4 %fusion.78 = (bf16[4,256,256]{1,2,0:T(8,128)(2,1)S(1)}, f32[4,256,256]{1,2,0:T(8,128)S(1)}, f32[4,256,256]{1,2,0:T(8,128)S(1)}) fusion(f32[4,256]{1,0:T(4,128)S(1)} %bitcast.219, bf16[4,4096,256]{2,1,0:T(8,128)(2,1)} %bitcast.225, f32[256,4096]{1,0:T(8,128)} %fusion.6), kind=kOutput, calls=%fused_computation.144 | convolution fusion | flops 2153250816 | bytes 15208448 | tf_op jit(solution)/shard_map/sd,tdh->tsh/dot_general | solution.py:436
  133.7 9.4 %collective-permute-start.17 = (bf16[256,256]{0,1:T(8,128)(2,1)S(1)}, bf16[256,256]{0,1:T(8,128)(2,1)S(1)}, u32[]{:S(2)}, u32[]{:S(2)}) collective-permute-start(bf16[256,256]{0,1:T(8,128)(2,1)S(1)} %get-tuple-element.30), channel_id=1, source_target_pairs={{0,2},{2,4},{4,6},{6,0},{1,3},{3,5},{5,7},{7,1},{8,10},{10,12},{12... | collective-permute-start | bytes 393224 | tf_op jit(solution)/shard_map/ppermute | solution.py:277
  146.9 4.1 %collective-permute-done.17 = bf16[256,256]{0,1:T(8,128)(2,1)S(1)} collective-permute-done((bf16[256,256]{0,1:T(8,128)(2,1)S(1)}, bf16[256,256]{0,1:T(8,128)(2,1)S(1)}, u32[]{:S(2)}, u32[]{:S(2)}) %collective-permute-start.17) | collective-permute-done | bytes 131104 | tf_op jit(solution)/shard_map/ppermute | solution.py:277
  155.4 3.9 %collective-permute-start.21 = (bf16[256,256]{0,1:T(8,128)(2,1)S(1)}, bf16[256,256]{0,1:T(8,128)(2,1)S(1)}, u32[]{:S(2)}, u32[]{:S(2)}) collective-permute-start(bf16[256,256]{0,1:T(8,128)(2,1)S(1)} %get-tuple-element.14), channel_id=1, source_target_pairs={{0,4},{2,6},{4,0},{6,2},{1,5},{3,7},{5,1},{7,3},{8,12},{10,14},{12... | collective-permute-start | bytes 393224 | tf_op jit(solution)/shard_map/ppermute | solution.py:277
  161.3 3.2 collective-permute-done.21
  165.4 8.7 %fusion.5 = f32[256,512]{1,0:T(8,128)} fusion(bf16[256,4096]{1,0:T(8,128)(2,1)} %copy-done.8, bf16[256,4096]{1,0:T(8,128)(2,1)} %copy-done.7, bf16[4,4096,256]{2,1,0:T(8,128)(2,1)} %bitcast.227, f32[256,4096]{1,0:T(8,128)} %fusion.6, f32[4,256]{1,0:T(4,128)} %bitcast.220, bf16[1,256,256]{1,2,0:T(8,128)(2,1)} %get-tuple-element.27, ...), kind=kOutput, calls=%fused_computation.13 | convolution fusion | flops 3240624128 | bytes 17829888 | tf_op jit(solution)/shard_map/dot_general | solution.py:39
  176.7 6.4 %fusion.19 = f32[32,4,8,128]{3,2,1,0:T(8,128)S(1)} fusion(f32[256,512]{1,0:T(8,128)S(1)} %fusion.51, f32[256,512]{1,0:T(8,128)} %fusion.5, bf16[256,4096]{1,0:T(8,128)(2,1)} %get-tuple-element.20, bf16[256,4096]{1,0:T(8,128)(2,1)S(1)} %get-tuple-element.19, f32[256,4096]{1,0:T(8,128)} %copy-done.28, bf16[4,4096,256]{2,1,0:T(8,128)(2,1)} %bitcast.228, ...), kind=kOutput, calls=%fused_computation.33 | convolution fusion | flops 1628897280 | bytes 12190724 | tf_op jit(solution)/shard_map/dot_general | solution.py:39
  183.6 3.2 collective-permute-start.24
  196.3 3.6 %collective-permute-start.29 = (bf16[4,256,128]{2,1,0:T(8,128)(2,1)S(1)}, bf16[4,256,128]{2,1,0:T(8,128)(2,1)S(1)}, u32[]{:S(2)}, u32[]{:S(2)}) collective-permute-start(bf16[4,256,128]{2,1,0:T(8,128)(2,1)S(1)} %pad_maximum_fusion.17.refs_0_), channel_id=1, source_target_pairs={{0,32},{8,40},{16,48},{24,56},{32,64},{40,72},{48,80},{56,88},{64,... | collective-permute-start | bytes 786440 | tf_op jit(solution)/shard_map/ppermute | solution.py:291
  199.9 3.3 collective-permute-done.29.refs_0_
  206.3 4.9 %collective-permute-done.30.refs_0_ = bf16[4,256,128]{2,1,0:T(8,128)(2,1)S(1)} collective-permute-done((bf16[4,256,128]{2,1,0:T(8,128)(2,1)S(1)}, bf16[4,256,128]{2,1,0:T(8,128)(2,1)S(1)}, u32[]{:S(2)}, u32[]{:S(2)}) %collective-permute-start.30) | collective-permute-done | bytes 262176 | tf_op jit(solution)/shard_map/ppermute | solution.py:291
  214.4 10.2 %collective-permute-start.44 = (bf16[4,256,128]{2,1,0:T(8,128)(2,1)S(1)}, bf16[4,256,128]{2,1,0:T(8,128)(2,1)S(1)}, u32[]{:S(2)}, u32[]{:S(2)}) collective-permute-start(bf16[4,256,128]{2,1,0:T(8,128)(2,1)S(1)} %pad_maximum_fusion.17.refs_0_), channel_id=1, source_target_pairs={{0,1},{1,0},{2,3},{3,2},{4,5},{5,4},{6,7},{7,6},{8,9},{9,8},{10,11... | collective-permute-start | bytes 786440 | tf_op jit(solution)/shard_map/ppermute | solution.py:281
  230.2 4.8 %collective-permute-start.40 = (bf16[4,256,128]{2,1,0:T(8,128)(2,1)S(1)}, bf16[4,256,128]{2,1,0:T(8,128)(2,1)S(1)}, u32[]{:S(2)}, u32[]{:S(2)}) collective-permute-start(bf16[4,256,128]{2,1,0:T(8,128)(2,1)S(1)} %collective-permute-done.30.refs_0_), channel_id=1, source_target_pairs={{0,1},{1,0},{2,3},{3,2},{4,5},{5,4},{6,7},{7,6},{8,9},{9,8},{10,11... | collective-permute-start | bytes 786440 | tf_op jit(solution)/shard_map/ppermute | solution.py:281
  236.6 44.7 %all-gather.1 = s32[64,1,192]{2,1,0:T(1,128)S(1)} all-gather(s32[1,1,192]{2,1,0:T(1,128)S(1)} %slice_bitcast_fusion.1), channel_id=1, replica_groups=mesh['table'=32,'task'=4,'fsdp'=2] {'table','fsdp'}, dimensions={0}, use_global_device_ids=true | all-gather | bytes 49920 | tf_op jit(solution)/shard_map/all_gather | solution.py:404
  281.9 5.5 %shard_map.116 = (s32[96,128]{1,0:T(8,128)S(1)}, s32[96,128]{1,0:T(8,128)S(1)}) custom-call(s32[96,128]{1,0:T(8,128)S(1)} %reshape.90.code_ref, bf16[256,64]{1,0:T(8,128)(2,1)S(1)} %pad_maximum_fusion.20.map_ref), custom_call_target="tpu_custom_call" | custom-call | tf_op jit(solution)/shard_map/pallas_call | solution.py:409
  287.5 6.1 %shard_map.117.refs_4_ = f32[4096,128]{1,0:T(8,128)} custom-call(s32[4]{0:T(128)S(1)} %pad_add_fusion.1.place_ref, s32[32,3,128]{2,1,0:T(4,128)S(1)} %reshape.91.row_ref, s32[32,3,128]{2,1,0:T(4,128)S(1)} %reshape.92.samp_ref, bf16[4,256,128]{2,1,0:T(8,128)(2,1)S(1)} %pad_maximum_fusion.17.refs_0_, bf16[4,256,128]{2,1,0:T(8,128)(2,1)S(1)} %collective-permute-done.44.refs_1_), custom_call_target="tpu_custom_call" | custom-call | tf_op jit(solution)/shard_map/pallas_call | solution.py:256
  293.5 11.2 %shard_map.118.refs_4_ = f32[4096,128]{1,0:T(8,128)} custom-call(s32[4]{0:T(128)S(1)} %pad_add_fusion.1.place_ref, s32[32,3,128]{2,1,0:T(4,128)S(1)} %reshape.91.row_ref, s32[32,3,128]{2,1,0:T(4,128)S(1)} %reshape.92.samp_ref, bf16[4,256,128]{2,1,0:T(8,128)(2,1)S(1)} %collective-permute-done.29.refs_0_, ...), custom_call_target="tpu_custom_call", output_to_operand_aliasing={{}: (7, {})} | custom-call | tf_op jit(solution)/shard_map/pallas_call | solution.py:256
  304.7 11.3 %shard_map.119.refs_4_ = f32[4096,128]{1,0:T(8,128)} custom-call(s32[4]{0:T(128)S(1)} %pad_add_fusion.1.place_ref, s32[32,3,128]{2,1,0:T(4,128)S(1)} %reshape.91.row_ref, s32[32,3,128]{2,1,0:T(4,128)S(1)} %reshape.92.samp_ref, bf16[4,256,128]{2,1,0:T(8,128)(2,1)S(1)} %collective-permute-done.30.refs_0_, ...), custom_call_target="tpu_custom_call", output_to_operand_aliasing={{}: (7, {})} | custom-call | tf_op jit(solution)/shard_map/pallas_call | solution.py:256
  316.0 11.4 %shard_map.120.refs_2_ = f32[4096,128]{1,0:T(8,128)} custom-call(s32[4]{0:T(128)S(1)} %pad_add_fusion.1.place_ref, s32[32,3,128]{2,1,0:T(4,128)S(1)} %reshape.91.row_ref, s32[32,3,128]{2,1,0:T(4,128)S(1)} %reshape.92.samp_ref, bf16[4,256,128]{2,1,0:T(8,128)(2,1)S(1)} %collective-permute-done.31.refs_0_, ...), custom_call_target="tpu_custom_call", output_to_operand_aliasing={{}: (7, {})} | custom-call | tf_op jit(solution)/shard_map/pallas_call | solution.py:256
  327.5 7.2 %shard_map.121 = f32[4096,128]{1,0:T(8,128)} custom-call(s32[4]{0:T(128)S(1)} %pad_add_fusion.1.place_ref, s32[32,3,128]{2,1,0:T(4,128)S(1)} %reshape.91.row_ref, s32[32,3,128]{2,1,0:T(4,128)S(1)} %reshape.92.samp_ref, bf16[4,256,128]{2,1,0:T(8,128)(2,1)S(1)} %constant_dynamic-update-slice_fusion.refs_0_, ...), custom_call_target="tpu_custom_call", output_to_operand_aliasing={{}: (5, {})} | custom-call | tf_op jit(solution)/shard_map/pallas_call | solution.py:256
  (206 shorter events, 83.1 us)
Async XLA Ops:
  7.2 118.1 %all-gather.4.cloned.1.call-start = ((), (), s32[]{:S(2)}) async-start(), calls=%async_computation.2 | async-start | bytes 9437184 | tf_op jit(solution)/shard_map/all_gather | solution.py:322
  10.0 42.5 %collective-permute-start = (bf16[4,528,128]{2,1,0:T(8,128)(2,1)S(1)}, bf16[4,528,128]{2,1,0:T(8,128)(2,1)S(1)}, u32[]{:S(2)}, u32[]{:S(2)}) collective-permute-start(bf16[4,528,128]{2,1,0:T(8,128)(2,1)S(1)} %fusion.26), channel_id=1, source_target_pairs={{0,1},{1,0},{2,3},{3,2},{4,5},{5,4},{6,7},{7,6},{8,9},{9,8},{10,11... | collective-permute-start | bytes 1622024 | tf_op jit(solution)/shard_map/ppermute | solution.py:281
  14.4 20.1 %all-to-all-start = ((s32[64,1,64]{2,1,0:T(1,128)}), s32[64,1,64]{2,1,0:T(1,128)S(1)}, u32[]{:S(2)}, u32[]{:S(2)}) async-start(s32[64,1,64]{2,1,0:T(1,128)} %bitcast.7), calls=%async_computation | async-start | bytes 65536 | tf_op jit(solution)/shard_map/all_to_all | solution.py:357
  26.2 88.1 %collective-permute-start.16 = (bf16[256,4096]{1,0:T(8,128)(2,1)}, bf16[256,4096]{1,0:T(8,128)(2,1)}, u32[]{:S(2)}, u32[]{:S(2)}) collective-permute-start(bf16[256,4096]{1,0:T(8,128)(2,1)} %bitcast.184), channel_id=1, source_target_pairs={{0,1},{1,0},{2,3},{3,2},{4,5},{5,4},{6,7},{7,6},{8,9},{9,8},{10,11... | collective-permute-start | bytes 6291464 | tf_op jit(solution)/shard_map/ppermute | solution.py:281
  46.6 60.5 %all-to-all-start.1 = ((bf16[64,64,128]{2,1,0:T(8,128)(2,1)}), bf16[64,64,128]{2,1,0:T(8,128)(2,1)S(1)}, u32[]{:S(2)}, u32[]{:S(2)}) async-start(bf16[64,64,128]{2,1,0:T(8,128)(2,1)} %bitcast.11), calls=%async_computation.1 | async-start | bytes 2097152 | tf_op jit(solution)/shard_map/all_to_all | solution.py:387
  54.0 7.9 %collective-permute-start.2 = (bf16[528,128]{1,0:T(8,128)(2,1)S(1)}, bf16[528,128]{1,0:T(8,128)(2,1)S(1)}, u32[]{:S(2)}, u32[]{:S(2)}) collective-permute-start(bf16[528,128]{1,0:T(8,128)(2,1)S(1)} %get-tuple-element.24), channel_id=1, source_target_pairs={{0,16},{8,24},{16,0},{24,8},{32,48},{40,56},{48,32},{56,40},{64,80... | collective-permute-start | bytes 405512 | tf_op jit(solution)/shard_map/ppermute | solution.py:285
  54.7 10.9 %collective-permute-start.3 = (bf16[528,128]{1,0:T(8,128)(2,1)S(1)}, bf16[528,128]{1,0:T(8,128)(2,1)S(1)}, u32[]{:S(2)}, u32[]{:S(2)}) collective-permute-start(bf16[528,128]{1,0:T(8,128)(2,1)S(1)} %get-tuple-element.23), channel_id=1, source_target_pairs={{0,24},{8,0},{16,8},{24,16},{32,56},{40,32},{48,40},{56,48},{64,88... | collective-permute-start | bytes 405512 | tf_op jit(solution)/shard_map/ppermute | solution.py:285
  65.6 15.4 %collective-permute-start.4 = (bf16[528,128]{1,0:T(8,128)(2,1)S(1)}, bf16[528,128]{1,0:T(8,128)(2,1)S(1)}, u32[]{:S(2)}, u32[]{:S(2)}) collective-permute-start(bf16[528,128]{1,0:T(8,128)(2,1)S(1)} %fusion.41), channel_id=1, source_target_pairs={{0,32},{8,40},{16,48},{24,56},{32,64},{40,72},{48,80},{56,88},{64,... | collective-permute-start | bytes 405512 | tf_op jit(solution)/shard_map/ppermute | solution.py:291
  66.7 14.3 %collective-permute-start.5 = (bf16[528,128]{1,0:T(8,128)(2,1)S(1)}, bf16[528,128]{1,0:T(8,128)(2,1)S(1)}, u32[]{:S(2)}, u32[]{:S(2)}) collective-permute-start(bf16[528,128]{1,0:T(8,128)(2,1)S(1)} %fusion.41), channel_id=1, source_target_pairs={{0,224},{8,232},{16,240},{24,248},{32,0},{40,8},{48,16},{56,24},{6... | collective-permute-start | bytes 405512 | tf_op jit(solution)/shard_map/ppermute | solution.py:291
  81.1 12.4 %collective-permute-start.6 = (bf16[528,128]{1,0:T(8,128)(2,1)S(1)}, bf16[528,128]{1,0:T(8,128)(2,1)S(1)}, u32[]{:S(2)}, u32[]{:S(2)}) collective-permute-start(bf16[528,128]{1,0:T(8,128)(2,1)S(1)} %select_select_fusion.1), channel_id=1, source_target_pairs={{0,96},{8,104},{16,112},{24,120},{32,128},{40,136},{48,144},{56,15... | collective-permute-start | bytes 405512 | tf_op jit(solution)/shard_map/ppermute | solution.py:291
  84.3 9.2 %collective-permute-start.7 = (bf16[528,128]{1,0:T(8,128)(2,1)S(1)}, bf16[528,128]{1,0:T(8,128)(2,1)S(1)}, u32[]{:S(2)}, u32[]{:S(2)}) collective-permute-start(bf16[528,128]{1,0:T(8,128)(2,1)S(1)} %select_select_fusion.1), channel_id=1, source_target_pairs={{0,160},{8,168},{16,176},{24,184},{32,192},{40,200},{48,208},{56,2... | collective-permute-start | bytes 405512 | tf_op jit(solution)/shard_map/ppermute | solution.py:291
  85.7 32.4 %collective-permute-start.15 = (bf16[256,4096]{1,0:T(8,128)(2,1)}, bf16[256,4096]{1,0:T(8,128)(2,1)}, u32[]{:S(2)}, u32[]{:S(2)}) collective-permute-start(bf16[256,4096]{1,0:T(8,128)(2,1)} %bitcast.185), channel_id=1, source_target_pairs={{0,1},{1,0},{2,3},{3,2},{4,5},{5,4},{6,7},{7,6},{8,9},{9,8},{10,11... | collective-permute-start | bytes 6291464 | tf_op jit(solution)/shard_map/ppermute | solution.py:281
  109.2 10.8 %collective-permute-start.12 = (bf16[256,128]{1,0:T(8,128)(2,1)S(1)}, bf16[256,128]{1,0:T(8,128)(2,1)S(1)}, u32[]{:S(2)}, u32[]{:S(2)}) collective-permute-start(bf16[256,128]{1,0:T(8,128)(2,1)S(1)} %shard_map.115), channel_id=1, source_target_pairs={{0,2},{2,4},{4,6},{6,0},{1,3},{3,5},{5,7},{7,1},{8,10},{10,12},{12... | collective-permute-start | bytes 196616 | tf_op jit(solution)/shard_map/ppermute | solution.py:277
  110.6 9.4 %collective-permute-start.13 = (bf16[256,128]{1,0:T(8,128)(2,1)S(1)}, bf16[256,128]{1,0:T(8,128)(2,1)S(1)}, u32[]{:S(2)}, u32[]{:S(2)}) collective-permute-start(bf16[256,128]{1,0:T(8,128)(2,1)S(1)} %shard_map.115), channel_id=1, source_target_pairs={{0,4},{2,6},{4,0},{6,2},{1,5},{3,7},{5,1},{7,3},{8,12},{10,14},{12... | collective-permute-start | bytes 196616 | tf_op jit(solution)/shard_map/ppermute | solution.py:277
  133.7 17.3 %collective-permute-start.17 = (bf16[256,256]{0,1:T(8,128)(2,1)S(1)}, bf16[256,256]{0,1:T(8,128)(2,1)S(1)}, u32[]{:S(2)}, u32[]{:S(2)}) collective-permute-start(bf16[256,256]{0,1:T(8,128)(2,1)S(1)} %get-tuple-element.30), channel_id=1, source_target_pairs={{0,2},{2,4},{4,6},{6,0},{1,3},{3,5},{5,7},{7,1},{8,10},{10,12},{12... | collective-permute-start | bytes 393224 | tf_op jit(solution)/shard_map/ppermute | solution.py:277
  143.1 7.9 %collective-permute-start.18 = (bf16[256,256]{0,1:T(8,128)(2,1)S(1)}, bf16[256,256]{0,1:T(8,128)(2,1)S(1)}, u32[]{:S(2)}, u32[]{:S(2)}) collective-permute-start(bf16[256,256]{0,1:T(8,128)(2,1)S(1)} %get-tuple-element.32), channel_id=1, source_target_pairs={{0,4},{2,6},{4,0},{6,2},{1,5},{3,7},{5,1},{7,3},{8,12},{10,14},{12... | collective-permute-start | bytes 393224 | tf_op jit(solution)/shard_map/ppermute | solution.py:277
  143.9 7.1 %collective-permute-start.19 = (bf16[256,256]{0,1:T(8,128)(2,1)S(1)}, bf16[256,256]{0,1:T(8,128)(2,1)S(1)}, u32[]{:S(2)}, u32[]{:S(2)}) collective-permute-start(bf16[256,256]{0,1:T(8,128)(2,1)S(1)} %get-tuple-element.31), channel_id=1, source_target_pairs={{0,6},{2,0},{4,2},{6,4},{1,7},{3,1},{5,3},{7,5},{8,14},{10,8},{12,... | collective-permute-start | bytes 393224 | tf_op jit(solution)/shard_map/ppermute | solution.py:277
  155.4 9.0 %collective-permute-start.21 = (bf16[256,256]{0,1:T(8,128)(2,1)S(1)}, bf16[256,256]{0,1:T(8,128)(2,1)S(1)}, u32[]{:S(2)}, u32[]{:S(2)}) collective-permute-start(bf16[256,256]{0,1:T(8,128)(2,1)S(1)} %get-tuple-element.14), channel_id=1, source_target_pairs={{0,4},{2,6},{4,0},{6,2},{1,5},{3,7},{5,1},{7,3},{8,12},{10,14},{12... | collective-permute-start | bytes 393224 | tf_op jit(solution)/shard_map/ppermute | solution.py:277
  196.3 6.9 %collective-permute-start.29 = (bf16[4,256,128]{2,1,0:T(8,128)(2,1)S(1)}, bf16[4,256,128]{2,1,0:T(8,128)(2,1)S(1)}, u32[]{:S(2)}, u32[]{:S(2)}) collective-permute-start(bf16[4,256,128]{2,1,0:T(8,128)(2,1)S(1)} %pad_maximum_fusion.17.refs_0_), channel_id=1, source_target_pairs={{0,32},{8,40},{16,48},{24,56},{32,64},{40,72},{48,80},{56,88},{64,... | collective-permute-start | bytes 786440 | tf_op jit(solution)/shard_map/ppermute | solution.py:291
  203.2 8.0 %collective-permute-start.30 = (bf16[4,256,128]{2,1,0:T(8,128)(2,1)S(1)}, bf16[4,256,128]{2,1,0:T(8,128)(2,1)S(1)}, u32[]{:S(2)}, u32[]{:S(2)}) collective-permute-start(bf16[4,256,128]{2,1,0:T(8,128)(2,1)S(1)} %collective-permute-done.29.refs_0_), channel_id=1, source_target_pairs={{0,32},{8,40},{16,48},{24,56},{32,64},{40,72},{48,80},{56,88},{64,... | collective-permute-start | bytes 786440 | tf_op jit(solution)/shard_map/ppermute | solution.py:291
  205.1 8.3 %collective-permute-start.34 = (bf16[4,256,128]{2,1,0:T(8,128)(2,1)S(1)}, bf16[4,256,128]{2,1,0:T(8,128)(2,1)S(1)}, u32[]{:S(2)}, u32[]{:S(2)}) collective-permute-start(bf16[4,256,128]{2,1,0:T(8,128)(2,1)S(1)} %collective-permute-done.33.refs_2_), channel_id=1, source_target_pairs={{0,224},{8,232},{16,240},{24,248},{32,0},{40,8},{48,16},{56,24},{6... | collective-permute-start | bytes 786440 | tf_op jit(solution)/shard_map/ppermute | solution.py:291
  211.2 13.9 %collective-permute-start.31 = (bf16[4,256,128]{2,1,0:T(8,128)(2,1)S(1)}, bf16[4,256,128]{2,1,0:T(8,128)(2,1)S(1)}, u32[]{:S(2)}, u32[]{:S(2)}) collective-permute-start(bf16[4,256,128]{2,1,0:T(8,128)(2,1)S(1)} %collective-permute-done.30.refs_0_), channel_id=1, source_target_pairs={{0,32},{8,40},{16,48},{24,56},{32,64},{40,72},{48,80},{56,88},{64,... | collective-permute-start | bytes 786440 | tf_op jit(solution)/shard_map/ppermute | solution.py:291
  213.4 11.8 %collective-permute-start.35 = (bf16[4,256,128]{2,1,0:T(8,128)(2,1)S(1)}, bf16[4,256,128]{2,1,0:T(8,128)(2,1)S(1)}, u32[]{:S(2)}, u32[]{:S(2)}) collective-permute-start(bf16[4,256,128]{2,1,0:T(8,128)(2,1)S(1)} %collective-permute-done.34.refs_2_), channel_id=1, source_target_pairs={{0,224},{8,232},{16,240},{24,248},{32,0},{40,8},{48,16},{56,24},{6... | collective-permute-start | bytes 786440 | tf_op jit(solution)/shard_map/ppermute | solution.py:291
  214.4 21.5 %collective-permute-start.44 = (bf16[4,256,128]{2,1,0:T(8,128)(2,1)S(1)}, bf16[4,256,128]{2,1,0:T(8,128)(2,1)S(1)}, u32[]{:S(2)}, u32[]{:S(2)}) collective-permute-start(bf16[4,256,128]{2,1,0:T(8,128)(2,1)S(1)} %pad_maximum_fusion.17.refs_0_), channel_id=1, source_target_pairs={{0,1},{1,0},{2,3},{3,2},{4,5},{5,4},{6,7},{7,6},{8,9},{9,8},{10,11... | collective-permute-start | bytes 786440 | tf_op jit(solution)/shard_map/ppermute | solution.py:281
  224.6 11.4 %collective-permute-start.42 = (bf16[4,256,128]{2,1,0:T(8,128)(2,1)S(1)}, bf16[4,256,128]{2,1,0:T(8,128)(2,1)S(1)}, u32[]{:S(2)}, u32[]{:S(2)}) collective-permute-start(bf16[4,256,128]{2,1,0:T(8,128)(2,1)S(1)} %collective-permute-done.29.refs_0_), channel_id=1, source_target_pairs={{0,1},{1,0},{2,3},{3,2},{4,5},{5,4},{6,7},{7,6},{8,9},{9,8},{10,11... | collective-permute-start | bytes 786440 | tf_op jit(solution)/shard_map/ppermute | solution.py:281
  224.6 11.9 %collective-permute-start.43 = (bf16[4,256,128]{2,1,0:T(8,128)(2,1)S(1)}, bf16[4,256,128]{2,1,0:T(8,128)(2,1)S(1)}, u32[]{:S(2)}, u32[]{:S(2)}) collective-permute-start(bf16[4,256,128]{2,1,0:T(8,128)(2,1)S(1)} %collective-permute-done.33.refs_2_), channel_id=1, source_target_pairs={{0,1},{1,0},{2,3},{3,2},{4,5},{5,4},{6,7},{7,6},{8,9},{9,8},{10,11... | collective-permute-start | bytes 786440 | tf_op jit(solution)/shard_map/ppermute | solution.py:281
  225.9 9.2 %collective-permute-start.36 = (bf16[2,256,128]{2,1,0:T(8,128)(2,1)}, bf16[2,256,128]{2,1,0:T(8,128)(2,1)S(1)}, u32[]{:S(2)}, u32[]{:S(2)}) collective-permute-start(bf16[2,256,128]{2,1,0:T(8,128)(2,1)} %slice.29), channel_id=1, source_target_pairs={{0,224},{8,232},{16,240},{24,248},{32,0},{40,8},{48,16},{56,24},{6... | collective-permute-start | bytes 393224 | tf_op jit(solution)/shard_map/ppermute | solution.py:291
  230.2 74.5 %collective-permute-start.40 = (bf16[4,256,128]{2,1,0:T(8,128)(2,1)S(1)}, bf16[4,256,128]{2,1,0:T(8,128)(2,1)S(1)}, u32[]{:S(2)}, u32[]{:S(2)}) collective-permute-start(bf16[4,256,128]{2,1,0:T(8,128)(2,1)S(1)} %collective-permute-done.30.refs_0_), channel_id=1, source_target_pairs={{0,1},{1,0},{2,3},{3,2},{4,5},{5,4},{6,7},{7,6},{8,9},{9,8},{10,11... | collective-permute-start | bytes 786440 | tf_op jit(solution)/shard_map/ppermute | solution.py:281
  235.0 69.7 %collective-permute-start.41 = (bf16[4,256,128]{2,1,0:T(8,128)(2,1)S(1)}, bf16[4,256,128]{2,1,0:T(8,128)(2,1)}, u32[]{:S(2)}, u32[]{:S(2)}) collective-permute-start(bf16[4,256,128]{2,1,0:T(8,128)(2,1)S(1)} %collective-permute-done.34.refs_2_), channel_id=1, source_target_pairs={{0,1},{1,0},{2,3},{3,2},{4,5},{5,4},{6,7},{7,6},{8,9},{9,8},{10,11... | collective-permute-start | bytes 786440 | tf_op jit(solution)/shard_map/ppermute | solution.py:281
  235.9 80.2 %collective-permute-start.38 = (bf16[4,256,128]{2,1,0:T(8,128)(2,1)S(1)}, bf16[4,256,128]{2,1,0:T(8,128)(2,1)}, u32[]{:S(2)}, u32[]{:S(2)}) collective-permute-start(bf16[4,256,128]{2,1,0:T(8,128)(2,1)S(1)} %collective-permute-done.31.refs_0_), channel_id=1, source_target_pairs={{0,1},{1,0},{2,3},{3,2},{4,5},{5,4},{6,7},{7,6},{8,9},{9,8},{10,11... | collective-permute-start | bytes 786440 | tf_op jit(solution)/shard_map/ppermute | solution.py:281
  236.0 80.1 %collective-permute-start.39 = (bf16[4,256,128]{2,1,0:T(8,128)(2,1)S(1)}, bf16[4,256,128]{2,1,0:T(8,128)(2,1)}, u32[]{:S(2)}, u32[]{:S(2)}) collective-permute-start(bf16[4,256,128]{2,1,0:T(8,128)(2,1)S(1)} %collective-permute-done.35.refs_2_), channel_id=1, source_target_pairs={{0,1},{1,0},{2,3},{3,2},{4,5},{5,4},{6,7},{7,6},{8,9},{9,8},{10,11... | collective-permute-start | bytes 786440 | tf_op jit(solution)/shard_map/ppermute | solution.py:281
  236.5 91.0 %collective-permute-start.37 = (bf16[4,256,128]{2,1,0:T(8,128)(2,1)S(1)}, bf16[4,256,128]{2,1,0:T(8,128)(2,1)}, u32[]{:S(2)}, u32[]{:S(2)}) collective-permute-start(bf16[4,256,128]{2,1,0:T(8,128)(2,1)S(1)} %constant_dynamic-update-slice_fusion.refs_0_), channel_id=1, source_target_pairs={{0,1},{1,0},{2,3},{3,2},{4,5},{5,4},{6,7},{7,6},{8,9},{9,8},{10,11... | collective-permute-start | bytes 786440 | tf_op jit(solution)/shard_map/ppermute | solution.py:281
  (45 other events, 480.2 us)
Sparse Core Ops, SparseCore 0:
  9.9 55.6 all-gather.3
